TPU v7x, 32 devices: a whole 2x2x4 slice. The times are simulated.
32 devices in a mesh: group: 2 (over y), wide: 8 (over z, x), narrow: 2 (over core).
Axes of the slice: x: 2, y: 2, z: 4, core: 2. Of those that a mesh axis runs over, the one named last changes fastest.
Arguments:
- hidden_in: bfloat16 [16, 16384], P(('group', 'wide'), 'narrow'), parts along dimension 0, may hold values from -60 to 60
- norm_gain: float32 [16384], P('narrow'), may hold values from 0.1 to 1.9
- qkv_weight: bfloat16 [16384, 9216], P('narrow', 'wide'), may hold values from -0.046875 to 0.046875
- out_weight: bfloat16 [8192, 16384], P('narrow', 'wide'), may hold values from -0.25 to 0.25
- cache_keys: bfloat16 [16, 256, 512], P(('group', 'wide'), None, 'narrow'), parts along dimension 0, may hold values from -500 to 500
- cache_values: bfloat16 [16, 256, 512], P(('group', 'wide'), None, 'narrow'), parts along dimension 0, may hold values from -6 to 6
- cache_lengths: int32 [16], P(('group', 'wide')), parts along dimension 0, may hold values from 4 to 256, as said below
Outputs:
- layer_out: float32 [16, 16384], P(('group', 'wide'), 'narrow'), parts along dimension 0
There are 2 independent parts, one for each index of `group`. A program takes and returns all parts, laid end to end along the dimension named above; an argument that names none is the same for every part. Nothing has to cross between parts.
Inputs may be any that keep to these rules, and one draw needn't show every extreme that they name: Some row's length is exactly 256 in every draw; row r's cached positions are 0 to cache_lengths[r] - 1 and its new token stands at position cache_lengths[r].
All inputs are finite; a program needn't handle non-finite values.
Results may differ from a plain program's by a relative error of at most 0.0058.
Values may be sent and summed in bfloat16 or wider, within the bound.
A program may use at most 64 MiB of HBM per device.

v0:
```python
import jax
import jax.numpy as jnp
from jax import lax
from jax.sharding import PartitionSpec as P

D = 16384
HD = 128


rope_theta = 500000.0
norm_eps = 1e-05


def rotary(values, position):
    half = values.shape[-1] // 2
    frequency = rope_theta ** (-jnp.arange(half, dtype=jnp.float32) * 2.0 / values.shape[-1])
    angles = position[..., None] * frequency
    cosine = jnp.cos(angles)
    sine = jnp.sin(angles)
    first = values[..., :half]
    second = values[..., half:]
    return jnp.concatenate([first * cosine - second * sine, second * cosine + first * sine], -1)


def attend(joined, keys, values, lengths):
    count = joined.shape[0]
    groups = joined.shape[1]
    share = joined.shape[2] - 2
    head_dim = joined.shape[3]
    capacity = keys.shape[1]
    position = lengths.astype(jnp.float32)
    query = (rotary(joined[:, :, :share], position[:, None, None]) * head_dim ** (-0.5)).astype(
        jnp.bfloat16
    )
    new_key = rotary(joined[:, :, share], position[:, None]).astype(jnp.bfloat16)
    new_value = joined[:, :, share + 1].astype(jnp.bfloat16)
    keys_four = keys.reshape(count, capacity, groups, head_dim)
    values_four = values.reshape(count, capacity, groups, head_dim)
    scores = jnp.einsum("bgjd,btgd->bgjt", query, keys_four, preferred_element_type=jnp.float32)
    own = jnp.sum(query.astype(jnp.float32) * new_key.astype(jnp.float32)[:, :, None, :], -1)
    live = jnp.arange(capacity)[None, None, None, :] < lengths[:, None, None, None]
    scores = jnp.where(live, scores, -1e30)
    top = jnp.maximum(jnp.max(scores, -1), own)
    expo = jnp.exp(scores - top[..., None])
    own_expo = jnp.exp(own - top)
    total = jnp.sum(expo, -1) + own_expo
    probs = (expo / total[..., None]).astype(jnp.bfloat16)
    mixed = jnp.einsum("bgjt,btgd->bgjd", probs, values_four, preferred_element_type=jnp.float32)
    mixed = mixed + (own_expo / total)[..., None] * new_value.astype(jnp.float32)[:, :, None, :]
    return mixed.astype(jnp.bfloat16).reshape(count, groups * share * head_dim)


def body(hidden_in, norm_gain, qkv_weight, out_weight, cache_keys, cache_values, cache_lengths):
    inputs = hidden_in.astype(jnp.float32)
    row_count = hidden_in.shape[0]
    squares = lax.psum(jnp.sum(inputs * inputs, -1), "narrow")
    normed = (inputs * lax.rsqrt(squares / D + norm_eps)[:, None] * norm_gain).astype(jnp.bfloat16)
    partial_qkv = jnp.dot(
        lax.all_gather(normed, "wide", axis=0, tiled=True),
        qkv_weight,
        preferred_element_type=jnp.float32,
    )
    all_rows, col_block = partial_qkv.shape
    halves = partial_qkv.reshape(all_rows, 1, 2, col_block // 2)
    paired = lax.psum_scatter(halves, "narrow", scatter_dimension=2, tiled=True)
    moved = lax.all_to_all(paired, "wide", split_axis=0, concat_axis=1, tiled=True)
    blocks = moved.shape[1]
    parted = moved.reshape(row_count, 2, blocks // 2, 1, col_block // 2)
    owned = lax.all_to_all(parted, "narrow", split_axis=1, concat_axis=3, tiled=True)
    owned = owned.reshape(row_count, blocks // 2 * col_block)
    groups = cache_keys.shape[2] // HD
    owned = owned.reshape(row_count, groups, owned.shape[1] // (groups * HD), HD)
    mixed = attend(owned, cache_keys, cache_values, cache_lengths)
    partial_out = jnp.dot(
        lax.all_gather(mixed, "wide", axis=0, tiled=True),
        out_weight,
        preferred_element_type=jnp.float32,
    )
    all_rows, col_block = partial_out.shape
    halves = partial_out.reshape(all_rows, 1, 2, col_block // 2)
    paired = lax.psum_scatter(halves, "narrow", scatter_dimension=2, tiled=True)
    moved = lax.all_to_all(paired, "wide", split_axis=0, concat_axis=1, tiled=True)
    blocks = moved.shape[1]
    parted = moved.reshape(row_count, 2, blocks // 2, 1, col_block // 2)
    added = lax.all_to_all(parted, "narrow", split_axis=1, concat_axis=3, tiled=True)
    added = added.reshape(row_count, blocks // 2 * col_block)
    return inputs + added


def solution(mesh):
    placed = (
        P(("group", "wide"), "narrow"),
        P("narrow"),
        P("narrow", "wide"),
        P("narrow", "wide"),
        P(("group", "wide"), None, "narrow"),
        P(("group", "wide"), None, "narrow"),
        P(("group", "wide")),
    )
    return jax.shard_map(
        body, mesh=mesh, in_specs=placed, out_specs=P(("group", "wide"), "narrow"), check_vma=False
    )
```

profile of v0, /device:TPU:0, one launch (start us, length us, event | category | flops | bytes accessed | tf_op | source)
XLA Modules:
  0.0 149.3 jit_solution(13513085413637469094)
XLA Ops:
  6.5 0.0 copy-start.1
  6.5 0.0 copy-start.2
  6.5 0.0 reduce-scatter.8.cloned.1.call-start
  6.5 1.5 multiply_reduce_fusion
  8.0 3.2 %psum.7 = f32[1]{0:T(128)} all-reduce(f32[1]{0:T(128)} %bitcast.1), channel_id=1, replica_groups=mesh['group'=2,'wide'=8,'narrow'=2] {'narrow'}, use_global_device_ids=true, to_apply=%region_1.0 | all-reduce | flops 1 | bytes 8 | tf_op jit(solution)/shard_map/psum | solution.py:56
  11.9 0.8 convert_bitcast_fusion
  12.7 32.4 %all-gather = bf16[8,1,8192]{2,1,0:T(2,128)(2,1)S(1)} all-gather(bf16[1,1,8192]{2,1,0:T(2,128)(2,1)S(1)} %convert_bitcast_fusion), channel_id=1, replica_groups=mesh['group'=2,'wide'=8,'narrow'=2] {'wide'}, dimensions={0}, use_global_device_ids=true | all-gather | bytes 147456 | tf_op jit(solution)/shard_map/all_gather | solution.py:59
  45.1 7.7 %fusion.1 = f32[8,1152]{1,0:T(8,128)S(1)} fusion(bf16[8192,1152]{1,0:T(8,128)(2,1)} %param.9, bf16[8,1,8192]{2,1,0:T(2,128)(2,1)S(1)} %all-gather), kind=kOutput, calls=%fused_computation.3 | convolution fusion | flops 150994944 | bytes 19042304 | tf_op jit(solution)/shard_map/dot_general | solution.py:58
  52.8 0.0 copy-start
  52.9 0.1 reshape.240
  52.9 0.6 copy.38
  53.6 0.0 reduce-scatter.8.cloned.1.call-update
  54.2 0.1 fusion.19
  54.3 7.8 %reduce-scatter.8.cloned.1.call-done = f32[8,1,1,576]{3,0,1,2:T(8,128)} async-done(((f32[8,1,2,576]{3,0,1,2:T(8,128)}), f32[8,1,1,576]{3,0,1,2:T(8,128)}) %reduce-scatter.8.cloned.1.call-update) | async-done | bytes 18448
  62.1 1.4 copy.39
  63.5 5.7 %all-to-all-start = ((f32[8,1,1,576]{3,2,1,0:T(1,128)}), f32[8,1,1,576]{3,2,1,0:T(1,128)S(1)}, u32[]{:S(2)}, u32[]{:S(2)}) async-start(f32[8,1,1,576]{3,2,1,0:T(1,128)} %copy.39), calls=%async_computation | async-start | bytes 40960 | tf_op jit(solution)/shard_map/all_to_all | solution.py:66
  69.2 0.0 reduce-scatter.6.cloned.1.call-start
  69.3 0.0 copy-done.1
  69.3 0.0 copy-done.2
  69.3 6.4 %all-to-all-done = f32[8,1,1,576]{3,2,1,0:T(1,128)S(1)} async-done(((f32[8,1,1,576]{3,2,1,0:T(1,128)}), f32[8,1,1,576]{3,2,1,0:T(1,128)S(1)}, u32[]{:S(2)}, u32[]{:S(2)}) %all-to-all-start) | async-done | bytes 18464 | tf_op jit(solution)/shard_map/all_to_all | solution.py:66
  75.8 3.7 %all_to_all.48 = f32[1,2,4,1,576]{4,3,2,0,1:T(1,128)S(1)} all-to-all(f32[1,2,4,1,576]{4,3,2,0,1:T(1,128)S(1)} %bitcast.47), channel_id=1, replica_groups=mesh['group'=2,'wide'=8,'narrow'=2] {'narrow'}, dimensions={1} | all-to-all | bytes 36864 | tf_op jit(solution)/shard_map/all_to_all | solution.py:69
  79.5 0.1 reshape_reshape.3
  79.6 0.1 multiply_subtract_fusion
  79.7 0.1 fusion.17
  79.8 0.1 maximum_convert_fusion
  79.9 0.2 multiply_reduce_fusion.1
  80.0 0.3 fusion.25
  80.3 0.2 fusion.9
  80.5 0.2 fusion
  80.7 30.6 %all-gather.1 = bf16[8,1,4096]{2,1,0:T(2,128)(2,1)S(1)} all-gather(bf16[1,1,4096]{2,1,0:T(2,128)(2,1)S(1)} %reshape.251), channel_id=1, replica_groups=mesh['group'=2,'wide'=8,'narrow'=2] {'wide'}, dimensions={0}, use_global_device_ids=true | all-gather | bytes 73728 | tf_op jit(solution)/shard_map/all_gather | solution.py:75
  111.3 8.7 %fusion.6 = f32[8,2048]{1,0:T(8,128)} fusion(bf16[4096,2048]{1,0:T(8,128)(2,1)} %param.10, bf16[8,1,4096]{2,1,0:T(2,128)(2,1)S(1)} %all-gather.1), kind=kOutput, calls=%fused_computation.8 | convolution fusion | flops 134217728 | bytes 16908288 | tf_op jit(solution)/shard_map/dot_general | solution.py:74
  120.0 0.0 reduce-scatter.6.cloned.1.call-update
  120.0 4.9 %reduce-scatter.6.cloned.1.call-done = f32[8,1,1,1024]{3,0,1,2:T(8,128)} async-done(((f32[8,1,2,1024]{3,0,1,2:T(8,128)}), f32[8,1,1,1024]{3,0,1,2:T(8,128)}) %reduce-scatter.6.cloned.1.call-update) | async-done | bytes 32784 | tf_op jit(solution)/shard_map/reduce_scatter | solution.py:81
  124.9 0.8 copy.45
  125.7 12.2 %all_to_all.49 = f32[8,1,1,1024]{3,2,1,0:T(1,128)S(1)} all-to-all(f32[8,1,1,1024]{3,2,1,0:T(1,128)S(1)} %copy.45), channel_id=1, replica_groups=mesh['group'=2,'wide'=8,'narrow'=2] {'wide'}, dimensions={0} | all-to-all | bytes 65536 | tf_op jit(solution)/shard_map/all_to_all | solution.py:82
  137.9 3.7 %all_to_all.50 = f32[1,2,4,1,1024]{4,2,3,0,1:T(4,128)S(1)} all-to-all(f32[1,2,4,1,1024]{4,2,3,0,1:T(4,128)S(1)} %copy.46), channel_id=1, replica_groups=mesh['group'=2,'wide'=8,'narrow'=2] {'narrow'}, dimensions={1} | all-to-all | bytes 65536 | tf_op jit(solution)/shard_map/all_to_all | solution.py:85
  141.7 0.1 reshape.247
  141.8 0.0 copy-done
  141.8 0.7 convert_add_fusion
  (11 shorter events, 0.2 us)
Async XLA Ops:
  6.5 62.7 %copy-start.1 = (bf16[1,256,256]{2,1,0:T(8,128)(2,1)S(1)}, bf16[1,256,256]{2,1,0:T(8,128)(2,1)}, u32[]{:S(2)}) copy-start(bf16[1,256,256]{2,1,0:T(8,128)(2,1)} %param.11) | copy-start | bytes 393220
  6.5 62.8 %copy-start.2 = (bf16[1,256,256]{2,1,0:T(8,128)(2,1)S(1)}, bf16[1,256,256]{2,1,0:T(8,128)(2,1)}, u32[]{:S(2)}) copy-start(bf16[1,256,256]{2,1,0:T(8,128)(2,1)} %param.12) | copy-start | bytes 393220
  6.5 55.6 %reduce-scatter.8.cloned.1.call-start = ((), (), s32[]{:S(2)}) async-start(), calls=%async_computation.7 | async-start | bytes 61440
  52.8 88.9 %copy-start = (bf16[1,8192]{1,0:T(2,128)(2,1)S(1)}, bf16[1,8192]{1,0:T(2,128)(2,1)}, u32[]{:S(2)}) copy-start(bf16[1,8192]{1,0:T(2,128)(2,1)} %param.7) | copy-start | bytes 49156
  63.5 12.3 %all-to-all-start = ((f32[8,1,1,576]{3,2,1,0:T(1,128)}), f32[8,1,1,576]{3,2,1,0:T(1,128)S(1)}, u32[]{:S(2)}, u32[]{:S(2)}) async-start(f32[8,1,1,576]{3,2,1,0:T(1,128)} %copy.39), calls=%async_computation | async-start | bytes 40960 | tf_op jit(solution)/shard_map/all_to_all | solution.py:66
  69.2 55.7 %reduce-scatter.6.cloned.1.call-start = ((), (), s32[]{:S(2)}) async-start(), calls=%async_computation.6 | async-start | bytes 98304 | tf_op jit(solution)/shard_map/reduce_scatter | solution.py:81
Sparse Core Ops, SparseCore 0:
  53.7 8.3 reduce-scatter.7
  120.1 4.6 reduce-scatter.5
where the time goes:
time: 150 us; the launch traced here: 149 us
  blocking collectives  85.9 us (57%)
  waiting for transfers between devices  19.2 us (13%)
  matrix products  16.9 us (11%)
  between operations  14.8 us (10%)
  starting transfers between devices  5.77 us (4%)
  other arithmetic  3.6 us (2%)
  local copies, waits for them, and re-layouts  3.14 us (2%)
    all_gather x1, blocking collectives, body(): lax.all_gather(normed, 'wide', axis=0, tiled=True)  32.4 us
    all_gather x1, blocking collectives, body(): lax.all_gather(mixed, 'wide', axis=0, tiled=True)  30.6 us
    all_to_all x1, blocking collectives, body(): lax.all_to_all(paired, 'wide', split_axis=0, concat_axis=1, tiled=True)  12.2 us
    dot_general x1, matrix products, body(): jnp.dot(lax.all_gather(mixed, 'wide', axis=0, tiled=True), out_weight, pr...  8.68 us
    unnamed x3, waiting for transfers between devices  7.85 us
    dot_general x1, matrix products, body(): jnp.dot(lax.all_gather(normed, 'wide', axis=0, tiled=True), qkv_weight, p...  7.71 us
    all_to_all x2, blocking collectives, body(): lax.all_to_all(parted, 'narrow', split_axis=1, concat_axis=3, tiled=True)  7.46 us
    all_to_all x1, waiting for transfers between devices, body(): lax.all_to_all(paired, 'wide', split_axis=0, concat_axis=1, tiled=True)  6.45 us
  transfers between devices with their start and end apart: 3, of which 3 were waited for; matrix products, arithmetic and copies ran while one was open for 0% of the time, Pallas kernels for 0%

commit v1 on v0

--- a/solution.py
+++ b/solution.py
@@ -1,14 +1,314 @@
+import functools
+import math
+
 import jax
 import jax.numpy as jnp
 from jax import lax
+from jax.experimental import pallas as pl
+from jax.experimental.pallas import tpu as pltpu
 from jax.sharding import PartitionSpec as P
 
-D = 16384
 HD = 128
 
 
 rope_theta = 500000.0
 norm_eps = 1e-05
+MESH = pl.DeviceIdType.MESH
+
+
+PIECE = 1024
+STEP = 2048
+
+
+def decode_kernel(
+    wide, narrow, heads, groups, features,
+    h_hbm, g_hbm, len_ref, k_hbm, v_hbm, wq_hbm, wo_hbm, out_ref,
+    h_in, gain, keys, values, wq, wo, hf, hsend, hrec, xs, lhs, ssown, ssrec, psend, prec, joined,
+    msend, mrec, ms, lhs2, osend, orec,
+    in_sem, q_sem, w_sem, ss_s, ss_r, h_s, h_r, p_s, p_r, m_s, m_r, o_s, o_r,
+):
+    w = lax.axis_index("wide")
+    n = lax.axis_index("narrow")
+    share = wide // narrow
+    blocks = hf.shape[0]
+    depth, out_depth = wq.shape[0], wo.shape[0]
+    turns = [w] + [lax.rem(w + d, wide) for d in range(1, wide)]
+
+    def load(weights, held, sem, step):
+        for i in range(STEP // PIECE):
+            at = pl.ds(step * STEP + i * PIECE, PIECE)
+            pltpu.make_async_copy(weights.at[at, :], held.at[at, :], sem.at[step]).start()
+
+    def loaded(held, sem, step):
+        block = held.at[pl.ds(step * STEP, STEP), :]
+        pltpu.make_async_copy(block, block, sem.at[step]).wait()
+
+    h_copy = pltpu.make_async_copy(h_hbm, h_in, in_sem.at[0])
+    g_copy = pltpu.make_async_copy(g_hbm, gain, in_sem.at[1])
+    k_copy = pltpu.make_async_copy(k_hbm, keys, in_sem.at[2])
+    v_copy = pltpu.make_async_copy(v_hbm, values, in_sem.at[3])
+    h_copy.start()
+    g_copy.start()
+
+    barrier = pltpu.get_barrier_semaphore()
+    for d in range(wide):
+        for e in range(narrow):
+            if d or e:
+                pl.semaphore_signal(
+                    barrier, inc=1,
+                    device_id={"wide": turns[d], "narrow": lax.rem(n + e, narrow)},
+                    device_id_type=MESH,
+                )
+
+    for step in range(depth // STEP):
+        load(wq_hbm, wq, q_sem, step)
+
+    h_copy.wait()
+    wide_row = h_in[...].astype(jnp.float32)
+    for b in range(blocks):
+        hf[b : b + 1, :] = wide_row[:, b * HD : (b + 1) * HD]
+    own = hf[...]
+    squares = jnp.sum(own * own, axis=0, keepdims=True)
+    ssown[...] = squares
+    g_copy.wait()
+
+    pl.semaphore_wait(barrier, wide * narrow - 1)
+
+    ss_copies = []
+    for d in range(1, narrow):
+        copy = pltpu.make_async_remote_copy(
+            src_ref=ssown, dst_ref=ssrec.at[d],
+            send_sem=ss_s.at[d], recv_sem=ss_r.at[d],
+            device_id={"narrow": lax.rem(n + d, narrow)},
+            device_id_type=MESH,
+        )
+        copy.start()
+        ss_copies.append(copy)
+    for d in range(1, narrow):
+        ss_copies[d - 1].wait_recv()
+        squares = squares + ssrec[d]
+    scale = lax.rsqrt(jnp.sum(squares, axis=-1, keepdims=True) / features + norm_eps)
+    hsend[...] = (own * scale * gain[...]).astype(jnp.bfloat16)
+
+    def spread(source, target, send, recv):
+        for d in range(1, wide):
+            pltpu.make_async_remote_copy(
+                src_ref=source, dst_ref=target.at[w],
+                send_sem=send.at[0], recv_sem=recv.at[0],
+                device_id={"wide": turns[d]},
+                device_id_type=MESH,
+            ).start()
+        target[w] = source[...]
+
+    def wait_for(buffer, count, sem):
+        block = buffer.at[pl.ds(0, count)]
+        pltpu.make_async_copy(block, block, sem.at[0]).wait()
+
+    spread(hsend, hrec, h_s, h_r)
+    k_copy.start()
+    v_copy.start()
+    for step in range(out_depth // STEP):
+        load(wo_hbm, wo, w_sem, step)
+
+    position = len_ref[0].astype(jnp.float32)
+    lane = lax.broadcasted_iota(jnp.int32, (1, HD), 1)
+    turn = lax.rem(lane, HD // 2).astype(jnp.float32)
+    angles = position * jnp.exp(turn * (-2.0 / HD * math.log(rope_theta)))
+    cosine = jnp.cos(angles)
+    sine = jnp.where(lane < HD // 2, -jnp.sin(angles), jnp.sin(angles))
+
+    def multiply(rows_in, flat, left, held, sem):
+        count = rows_in.shape[1]
+        for s in range(wide):
+            flat[s * count : (s + 1) * count, :] = rows_in[s].astype(jnp.float32)
+        per = STEP // HD
+        total = None
+        for step in range(count // per):
+            for b in range(step * per, (step + 1) * per):
+                left[:, b * HD : (b + 1) * HD] = flat[
+                    pl.ds(b, wide, stride=count), :
+                ].astype(jnp.bfloat16)
+            loaded(held, sem, step)
+            at = slice(step * STEP, (step + 1) * STEP)
+            product = jnp.dot(left[:, at], held[at, :], preferred_element_type=jnp.float32)
+            total = product if total is None else total + product
+        return total
+
+    wait_for(hrec, wide - 1, h_r)
+    total = multiply(hrec, xs, lhs, wq, q_sem)
+    for j in range(heads):
+        psend[:, j, :] = total[:, j * HD : (j + 1) * HD]
+
+    slot = lax.rem(w, share) * narrow + n
+    owner = w // share
+
+    def collect(source, target, send, recv):
+        for d in range(wide):
+            copy = pltpu.make_async_remote_copy(
+                src_ref=source.at[turns[d]], dst_ref=target.at[slot],
+                send_sem=send.at[0], recv_sem=recv.at[0],
+                device_id={"wide": turns[d], "narrow": owner},
+                device_id_type=MESH,
+            )
+            if d:
+                copy.start()
+                continue
+
+            @pl.when(owner == n)
+            def _():
+                pltpu.make_async_copy(source.at[w], target.at[slot], recv.at[0]).start()
+
+            @pl.when(owner != n)
+            def _():
+                copy.start()
+
+    def added(target, b):
+        block = target[b * narrow]
+        for i in range(1, narrow):
+            block = block + target[b * narrow + i]
+        return block
+
+    collect(psend, prec, p_s, p_r)
+    k_copy.wait()
+    v_copy.wait()
+    wait_for(prec, wide, p_r)
+
+    per_group = share // groups
+    context = keys.shape[1]
+    queries = per_group * heads - 2
+    for g in range(groups):
+        for b in range(per_group):
+            joined[g, b * heads : (b + 1) * heads, :] = added(prec, g * per_group + b)
+    for g in range(groups):
+        turned = joined[g, 0 : queries, :]
+        turned = turned * cosine + pltpu.roll(turned, HD // 2, 1) * sine
+        query = (turned * HD ** (-0.5)).astype(jnp.bfloat16)
+        new_key = joined[g, queries : queries + 1, :]
+        new_key = new_key * cosine + pltpu.roll(new_key, HD // 2, 1) * sine
+        new_key = new_key.astype(jnp.bfloat16).astype(jnp.float32)
+        new_value = joined[g, queries + 1 : queries + 2, :].astype(jnp.bfloat16).astype(jnp.float32)
+        scores = lax.dot_general(
+            query, keys[0, :, g * HD : (g + 1) * HD], (((1,), (1,)), ((), ())),
+            preferred_element_type=jnp.float32,
+        )
+        own_score = jnp.sum(query.astype(jnp.float32) * new_key, axis=-1, keepdims=True)
+        live = lax.broadcasted_iota(jnp.int32, (queries, context), 1) < len_ref[0]
+        scores = jnp.where(live, scores, -1e30)
+        top = jnp.maximum(jnp.max(scores, axis=-1, keepdims=True), own_score)
+        expo = jnp.exp(scores - top)
+        own_expo = jnp.exp(own_score - top)
+        weight = jnp.sum(expo, axis=-1, keepdims=True) + own_expo
+        probs = (expo / weight).astype(jnp.bfloat16)
+        mixed = jnp.dot(
+            probs, values[0, :, g * HD : (g + 1) * HD], preferred_element_type=jnp.float32
+        )
+        mixed = mixed + (own_expo / weight) * new_value
+        msend[g * queries : (g + 1) * queries, :] = mixed.astype(jnp.bfloat16)
+
+    spread(msend, mrec, m_s, m_r)
+    wait_for(mrec, wide - 1, m_r)
+    total = multiply(mrec, ms, lhs2, wo, w_sem)
+    count = wo.shape[1] // HD
+    for j in range(count):
+        osend[:, j, :] = total[:, j * HD : (j + 1) * HD]
+    collect(osend, orec, o_s, o_r)
+    wait_for(orec, wide, o_r)
+    for b in range(share):
+        out_ref[b * count : (b + 1) * count, :] = added(orec, b)
+
+    for copy in ss_copies:
+        copy.wait_send()
+    wait_for(hrec, wide - 1, h_s)
+    wait_for(prec, wide - 1, p_s)
+    wait_for(mrec, wide - 1, m_s)
+    wait_for(orec, wide - 1, o_s)
+
+    @pl.when(owner != n)
+    def _():
+        wait_for(prec, 1, p_s)
+        wait_for(orec, 1, o_s)
+
+
+def fused(sizes, hidden_in, norm_gain, qkv_weight, out_weight, cache_keys, cache_values, cache_lengths):
+    wide, narrow = sizes
+    depth, columns = qkv_weight.shape
+    out_depth, out_columns = out_weight.shape
+    heads = columns // HD
+    groups = cache_keys.shape[2] // HD
+    blocks = depth // HD
+    out_blocks = out_columns // HD
+    share = wide // narrow
+    mixed_blocks = out_depth // HD
+    bf16, f32 = jnp.bfloat16, jnp.float32
+    dma = pltpu.SemaphoreType.DMA
+    anywhere = pl.BlockSpec(memory_space=pltpu.HBM)
+    out = pl.pallas_call(
+        functools.partial(decode_kernel, wide, narrow, heads, groups, depth * narrow),
+        out_shape=jax.ShapeDtypeStruct((blocks, HD), f32),
+        in_specs=[
+            anywhere, anywhere, pl.BlockSpec(memory_space=pltpu.SMEM),
+            anywhere, anywhere, anywhere, anywhere,
+        ],
+        out_specs=pl.BlockSpec(memory_space=pltpu.VMEM),
+        scratch_shapes=[
+            pltpu.VMEM(hidden_in.shape, bf16),
+            pltpu.VMEM((blocks, HD), f32),
+            pltpu.VMEM(cache_keys.shape, bf16),
+            pltpu.VMEM(cache_values.shape, bf16),
+            pltpu.VMEM((depth, columns), bf16),
+            pltpu.VMEM((out_depth, out_columns), bf16),
+            pltpu.VMEM((blocks, HD), f32),
+            pltpu.VMEM((blocks, HD), bf16),
+            pltpu.VMEM((wide, blocks, HD), bf16),
+            pltpu.VMEM((wide * blocks, HD), f32),
+            pltpu.VMEM((wide, depth), bf16),
+            pltpu.VMEM((1, HD), f32),
+            pltpu.VMEM((narrow, 1, HD), f32),
+            pltpu.VMEM((wide, heads, HD), f32),
+            pltpu.VMEM((wide, heads, HD), f32),
+            pltpu.VMEM((groups, share // groups * heads, HD), f32),
+            pltpu.VMEM((mixed_blocks, HD), bf16),
+            pltpu.VMEM((wide, mixed_blocks, HD), bf16),
+            pltpu.VMEM((wide * mixed_blocks, HD), f32),
+            pltpu.VMEM((wide, out_depth), bf16),
+            pltpu.VMEM((wide, out_blocks, HD), f32),
+            pltpu.VMEM((wide, out_blocks, HD), f32),
+            dma((4,)), dma((depth // STEP,)), dma((out_depth // STEP,)),
+            dma((narrow,)), dma((narrow,)),
+            dma((1,)), dma((1,)),
+            dma((1,)), dma((1,)),
+            dma((1,)), dma((1,)),
+            dma((1,)), dma((1,)),
+        ],
+        compiler_params=pltpu.CompilerParams(
+            collective_id=0, has_side_effects=True,
+            vmem_limit_bytes=63 * 1024 * 1024 + 768 * 1024,
+        ),
+        cost_estimate=pl.CostEstimate(
+            flops=2 * wide * (depth * columns + out_depth * out_columns),
+            bytes_accessed=2 * (depth * columns + out_depth * out_columns),
+            transcendentals=0,
+        ),
+        name="decode",
+    )(
+        hidden_in, norm_gain.reshape(blocks, HD), cache_lengths,
+        cache_keys, cache_values, qkv_weight, out_weight,
+    )
+    return hidden_in.astype(f32) + out.reshape(1, blocks * HD)
+
+
+def fits(sizes, hidden_in, qkv_weight, out_weight, cache_keys):
+    wide, narrow = sizes
+    columns = qkv_weight.shape[1]
+    groups = cache_keys.shape[2] // HD
+    if hidden_in.shape[0] != 1 or columns % HD or out_weight.shape[1] % (8 * HD):
+        return False
+    if wide % narrow or (wide // narrow) % groups or wide % 8:
+        return False
+    if qkv_weight.shape[0] % STEP or out_weight.shape[0] % STEP:
+        return False
+    queries = (wide // narrow) // groups * (columns // HD) - 2
+    return queries % 16 == 0 and queries * groups * HD == out_weight.shape[0]
 
 
 def rotary(values, position):
@@ -51,10 +351,16 @@
 
 
 def body(hidden_in, norm_gain, qkv_weight, out_weight, cache_keys, cache_values, cache_lengths):
+    sizes = [lax.axis_size(name) for name in ("wide", "narrow")]
+    if fits(sizes, hidden_in, qkv_weight, out_weight, cache_keys):
+        return fused(
+            sizes, hidden_in, norm_gain, qkv_weight, out_weight,
+            cache_keys, cache_values, cache_lengths,
+        )
     inputs = hidden_in.astype(jnp.float32)
     row_count = hidden_in.shape[0]
     squares = lax.psum(jnp.sum(inputs * inputs, -1), "narrow")
-    normed = (inputs * lax.rsqrt(squares / D + norm_eps)[:, None] * norm_gain).astype(jnp.bfloat16)
+    normed = (inputs * lax.rsqrt(squares / (hidden_in.shape[1] * sizes[1]) + norm_eps)[:, None] * norm_gain).astype(jnp.bfloat16)
     partial_qkv = jnp.dot(
         lax.all_gather(normed, "wide", axis=0, tiled=True),
         qkv_weight,

time: 150 us -> 32.9 us (0.22)
  blocking collectives: 85.9 us -> 0 us
  Pallas kernels: 0 us -> 30.4 us
  waiting for transfers between devices: 19.2 us -> 0 us
  matrix products: 16.9 us -> 0 us
  between operations: 14.8 us -> 0.68 us
  starting transfers between devices: 5.77 us -> 0 us
  local copies, waits for them, and re-layouts: 3.14 us -> 0.01 us
  other arithmetic: 3.6 us -> 1.42 us
    all_gather x2 -> x0, blocking collectives: 63 us -> none  [the longest x1 32.4 us: body(): lax.all_gather(normed, 'wide', axis=0, tiled=True)]
    pallas_call x0 -> x1, Pallas kernels: none -> 30.4 us  [fused(): pl.pallas_call(functools.partial(decode_kernel, wide, narrow, heads, grou...]
    all_to_all x3 -> x0, blocking collectives: 19.7 us -> none  [the longest x1 12.2 us: body(): lax.all_to_all(paired, 'wide', split_axis=0, concat_axis=1, tiled=True)]
    dot_general x4 -> x0, matrix products: 16.9 us -> none  [the longest x1 8.68 us: body(): jnp.dot(lax.all_gather(mixed, 'wide', axis=0, tiled=True), out_weight, pr...]
    unnamed x3 -> x0, waiting for transfers between devices: 7.85 us -> none
    all_to_all x1 -> x0, waiting for transfers between devices: 6.45 us -> none  [body(): lax.all_to_all(paired, 'wide', split_axis=0, concat_axis=1, tiled=True)]
    all_to_all x1 -> x0, starting transfers between devices: 5.73 us -> none  [body(): lax.all_to_all(paired, 'wide', split_axis=0, concat_axis=1, tiled=True)]
    reduce_scatter x1 -> x0, waiting for transfers between devices: 4.86 us -> none  [body(): paired = lax.psum_scatter(halves, 'narrow', scatter_dimension=2, tiled=True)]
  transfers between devices with their start and end apart: 3 -> 0, of which waited for: 3 -> 0; matrix products, arithmetic and copies ran while one was open for 0% -> 0% of each run, Pallas kernels for 0% -> 0%
where the time goes in v1:
time: 32.9 us; the launch traced here: 32.5 us
  Pallas kernels  30.4 us (92%)
  other arithmetic  1.42 us (4%)
  between operations  0.68 us (2%)
    pallas_call x1, Pallas kernels, fused(): pl.pallas_call(functools.partial(decode_kernel, wide, narrow, heads, grou...  30.4 us
    add x1, other arithmetic, fused(): return hidden_in.astype(f32) + out.reshape(1, blocks * HD)  1.42 us

profile of v1, /device:TPU:0, one launch (start us, length us, event | category | flops | bytes accessed | tf_op | source)
XLA Modules:
  0.0 32.5 jit_solution(6708343013001957457)
XLA Ops:
  0.0 0.0 copy-start
  0.7 30.4 %decode.1 = f32[64,128]{1,0:T(8,128)} custom-call(bf16[1,8192]{1,0:T(2,128)(2,1)} %h_hbm.1, f32[64,128]{1,0:T(8,128)} %bitcast.3, s32[1]{0:T(128)S(6)} %copy.8.len_ref, bf16[1,256,256]{2,1,0:T(8,128)(2,1)} %k_hbm.1, bf16[1,256,256]{2,1,0:T(8,128)(2,1)} %v_hbm.1, bf16[8192,1152]{1,0:T(8,128)(2,1)} %wq_hbm.1, bf16[4096,2048]{1,0:T(8,128)(2,1)} %wo_hbm.1), custom_call_target="tpu_custom_call" | custom-call | flops 285212672 | bytes 35651584 | tf_op jit(solution)/shard_map/decode/pallas_call | solution.py:245
  31.0 0.0 copy-done
  31.0 1.4 %convert_add_fusion = f32[1,8192]{1,0:T(1,128)} fusion(f32[1,8192]{1,0:T(1,128)} %bitcast.2, bf16[1,8192]{1,0:T(2,128)(2,1)S(1)} %copy-done), kind=kLoop, calls=%fused_computation | loop fusion | flops 16384 | bytes 81920 | tf_op jit(solution)/shard_map/add | solution.py:297
Async XLA Ops:
  0.0 31.0 %copy-start = (bf16[1,8192]{1,0:T(2,128)(2,1)S(1)}, bf16[1,8192]{1,0:T(2,128)(2,1)}, u32[]{:S(2)}) copy-start(bf16[1,8192]{1,0:T(2,128)(2,1)} %h_hbm.1) | copy-start | bytes 49156

commit v2 on v1

--- a/solution.py
+++ b/solution.py
@@ -16,6 +16,7 @@
 MESH = pl.DeviceIdType.MESH
 
 
+PARTS = 2
 PIECE = 1024
 STEP = 2048
 
@@ -23,7 +24,7 @@
 def decode_kernel(
     wide, narrow, heads, groups, features,
     h_hbm, g_hbm, len_ref, k_hbm, v_hbm, wq_hbm, wo_hbm, out_ref,
-    h_in, gain, keys, values, wq, wo, hf, hsend, hrec, xs, lhs, ssown, ssrec, psend, prec, joined,
+    h_in, gain, keys, values, wq, wo, hf, hsend, hrec, xs, lhs, ssrec, psend, prec, joined,
     msend, mrec, ms, lhs2, osend, orec,
     in_sem, q_sem, w_sem, ss_s, ss_r, h_s, h_r, p_s, p_r, m_s, m_r, o_s, o_r,
 ):
@@ -69,42 +70,40 @@
         hf[b : b + 1, :] = wide_row[:, b * HD : (b + 1) * HD]
     own = hf[...]
     squares = jnp.sum(own * own, axis=0, keepdims=True)
-    ssown[...] = squares
+    me = n * wide + w
+    ssrec[me] = squares
+    hsend[...] = own.astype(jnp.bfloat16)
     g_copy.wait()
 
     pl.semaphore_wait(barrier, wide * narrow - 1)
 
-    ss_copies = []
-    for d in range(1, narrow):
-        copy = pltpu.make_async_remote_copy(
-            src_ref=ssown, dst_ref=ssrec.at[d],
-            send_sem=ss_s.at[d], recv_sem=ss_r.at[d],
-            device_id={"narrow": lax.rem(n + d, narrow)},
-            device_id_type=MESH,
-        )
-        copy.start()
-        ss_copies.append(copy)
-    for d in range(1, narrow):
-        ss_copies[d - 1].wait_recv()
-        squares = squares + ssrec[d]
-    scale = lax.rsqrt(jnp.sum(squares, axis=-1, keepdims=True) / features + norm_eps)
-    hsend[...] = (own * scale * gain[...]).astype(jnp.bfloat16)
-
-    def spread(source, target, send, recv):
+    def spread(source, target, part, send, recv):
+        size = target.shape[2]
+        block = source.at[pl.ds(part * size, size)]
         for d in range(1, wide):
             pltpu.make_async_remote_copy(
-                src_ref=source, dst_ref=target.at[w],
-                send_sem=send.at[0], recv_sem=recv.at[0],
+                src_ref=block, dst_ref=target.at[part, w],
+                send_sem=send.at[part], recv_sem=recv.at[part],
                 device_id={"wide": turns[d]},
                 device_id_type=MESH,
             ).start()
-        target[w] = source[...]
+        target[part, w] = block[...]
 
     def wait_for(buffer, count, sem):
         block = buffer.at[pl.ds(0, count)]
-        pltpu.make_async_copy(block, block, sem.at[0]).wait()
-
-    spread(hsend, hrec, h_s, h_r)
+        pltpu.make_async_copy(block, block, sem).wait()
+
+    for d in range(wide):
+        for e in range(narrow):
+            if d or e:
+                pltpu.make_async_remote_copy(
+                    src_ref=ssrec.at[me], dst_ref=ssrec.at[me],
+                    send_sem=ss_s.at[0], recv_sem=ss_r.at[0],
+                    device_id={"wide": turns[d], "narrow": lax.rem(n + e, narrow)},
+                    device_id_type=MESH,
+                ).start()
+    for part in range(PARTS):
+        spread(hsend, hrec, part, h_s, h_r)
     k_copy.start()
     v_copy.start()
     for step in range(out_depth // STEP):
@@ -117,25 +116,30 @@
     cosine = jnp.cos(angles)
     sine = jnp.where(lane < HD // 2, -jnp.sin(angles), jnp.sin(angles))
 
-    def multiply(rows_in, flat, left, held, sem):
-        count = rows_in.shape[1]
+    wait_for(ssrec, wide * narrow - 1, ss_r.at[0])
+    squares = ssrec[0:wide]
+    for part in range(1, narrow):
+        squares = squares + ssrec[part * wide : (part + 1) * wide]
+    scale = lax.rsqrt(jnp.sum(squares, axis=-1, keepdims=True) / features + norm_eps)
+    per = STEP // HD
+    half = blocks // PARTS
+    total = None
+    for part in range(PARTS):
+        wait_for(hrec.at[part], wide - 1, h_r.at[part])
+        gains = gain[part * half : (part + 1) * half, :]
         for s in range(wide):
-            flat[s * count : (s + 1) * count, :] = rows_in[s].astype(jnp.float32)
-        per = STEP // HD
-        total = None
-        for step in range(count // per):
-            for b in range(step * per, (step + 1) * per):
-                left[:, b * HD : (b + 1) * HD] = flat[
-                    pl.ds(b, wide, stride=count), :
+            xs[s * half : (s + 1) * half, :] = hrec[part, s].astype(jnp.float32) * scale[s] * gains
+        for step in range(half // per):
+            for b in range(per):
+                lhs[:, b * HD : (b + 1) * HD] = xs[
+                    pl.ds(step * per + b, wide, stride=half), :
                 ].astype(jnp.bfloat16)
-            loaded(held, sem, step)
-            at = slice(step * STEP, (step + 1) * STEP)
-            product = jnp.dot(left[:, at], held[at, :], preferred_element_type=jnp.float32)
+            at = part * (half // per) + step
+            loaded(wq, q_sem, at)
+            product = jnp.dot(
+                lhs[...], wq[at * STEP : (at + 1) * STEP, :], preferred_element_type=jnp.float32
+            )
             total = product if total is None else total + product
-        return total
-
-    wait_for(hrec, wide - 1, h_r)
-    total = multiply(hrec, xs, lhs, wq, q_sem)
     for j in range(heads):
         psend[:, j, :] = total[:, j * HD : (j + 1) * HD]
 
@@ -146,7 +150,7 @@
         for d in range(wide):
             copy = pltpu.make_async_remote_copy(
                 src_ref=source.at[turns[d]], dst_ref=target.at[slot],
-                send_sem=send.at[0], recv_sem=recv.at[0],
+                send_sem=send, recv_sem=recv,
                 device_id={"wide": turns[d], "narrow": owner},
                 device_id_type=MESH,
             )
@@ -156,7 +160,7 @@
 
             @pl.when(owner == n)
             def _():
-                pltpu.make_async_copy(source.at[w], target.at[slot], recv.at[0]).start()
+                pltpu.make_async_copy(source.at[w], target.at[slot], recv).start()
 
             @pl.when(owner != n)
             def _():
@@ -168,10 +172,10 @@
             block = block + target[b * narrow + i]
         return block
 
-    collect(psend, prec, p_s, p_r)
+    collect(psend, prec, p_s.at[0], p_r.at[0])
     k_copy.wait()
     v_copy.wait()
-    wait_for(prec, wide, p_r)
+    wait_for(prec, wide, p_r.at[0])
 
     per_group = share // groups
     context = keys.shape[1]
@@ -204,29 +208,57 @@
         )
         mixed = mixed + (own_expo / weight) * new_value
         msend[g * queries : (g + 1) * queries, :] = mixed.astype(jnp.bfloat16)
-
-    spread(msend, mrec, m_s, m_r)
-    wait_for(mrec, wide - 1, m_r)
-    total = multiply(mrec, ms, lhs2, wo, w_sem)
-    count = wo.shape[1] // HD
-    for j in range(count):
-        osend[:, j, :] = total[:, j * HD : (j + 1) * HD]
-    collect(osend, orec, o_s, o_r)
-    wait_for(orec, wide, o_r)
-    for b in range(share):
-        out_ref[b * count : (b + 1) * count, :] = added(orec, b)
-
-    for copy in ss_copies:
-        copy.wait_send()
-    wait_for(hrec, wide - 1, h_s)
-    wait_for(prec, wide - 1, p_s)
-    wait_for(mrec, wide - 1, m_s)
-    wait_for(orec, wide - 1, o_s)
+        spread(msend, mrec, g, m_s, m_r)
+
+    deep = queries * HD
+    width = wo.shape[1] // PARTS
+    count = width // HD
+    total = None
+    for g in range(groups):
+        wait_for(mrec.at[g], wide - 1, m_r.at[g])
+        for s in range(wide):
+            ms[s * queries : (s + 1) * queries, :] = mrec[g, s].astype(jnp.float32)
+        for b in range(queries):
+            lhs2[:, b * HD : (b + 1) * HD] = ms[
+                pl.ds(b, wide, stride=queries), :
+            ].astype(jnp.bfloat16)
+        for step in range(g * deep // STEP, (g + 1) * deep // STEP):
+            loaded(wo, w_sem, step)
+        if g < groups - 1:
+            product = jnp.dot(
+                lhs2[...], wo[g * deep : (g + 1) * deep, :], preferred_element_type=jnp.float32
+            )
+            total = product if total is None else total + product
+            continue
+        for part in range(PARTS):
+            at = slice(part * width, (part + 1) * width)
+            product = jnp.dot(
+                lhs2[...], wo[g * deep : (g + 1) * deep, at], preferred_element_type=jnp.float32
+            )
+            if total is not None:
+                product = total[:, at] + product
+            for j in range(count):
+                osend[part, :, j, :] = product[:, j * HD : (j + 1) * HD]
+            collect(osend.at[part], orec.at[part], o_s.at[part], o_r.at[part])
+
+    for part in range(PARTS):
+        wait_for(orec.at[part], wide, o_r.at[part])
+        for b in range(share):
+            start = (b * PARTS + part) * count
+            out_ref[start : start + count, :] = hf[start : start + count, :] + added(orec.at[part], b)
+
+    wait_for(ssrec, wide * narrow - 1, ss_s.at[0])
+    sent = [(hrec.at[part], h_s.at[part]) for part in range(PARTS)]
+    sent += [(mrec.at[g], m_s.at[g]) for g in range(groups)]
+    shared = [(prec, p_s.at[0])]
+    shared += [(orec.at[part], o_s.at[part]) for part in range(PARTS)]
+    for buffer, sem in sent + shared:
+        wait_for(buffer, wide - 1, sem)
 
     @pl.when(owner != n)
     def _():
-        wait_for(prec, 1, p_s)
-        wait_for(orec, 1, o_s)
+        for buffer, sem in shared:
+            wait_for(buffer, 1, sem)
 
 
 def fused(sizes, hidden_in, norm_gain, qkv_weight, out_weight, cache_keys, cache_values, cache_lengths):
@@ -259,26 +291,25 @@
             pltpu.VMEM((out_depth, out_columns), bf16),
             pltpu.VMEM((blocks, HD), f32),
             pltpu.VMEM((blocks, HD), bf16),
-            pltpu.VMEM((wide, blocks, HD), bf16),
-            pltpu.VMEM((wide * blocks, HD), f32),
-            pltpu.VMEM((wide, depth), bf16),
-            pltpu.VMEM((1, HD), f32),
-            pltpu.VMEM((narrow, 1, HD), f32),
+            pltpu.VMEM((PARTS, wide, blocks // PARTS, HD), bf16),
+            pltpu.VMEM((wide * blocks // PARTS, HD), f32),
+            pltpu.VMEM((wide, STEP), bf16),
+            pltpu.VMEM((wide * narrow, 1, HD), f32),
             pltpu.VMEM((wide, heads, HD), f32),
             pltpu.VMEM((wide, heads, HD), f32),
             pltpu.VMEM((groups, share // groups * heads, HD), f32),
             pltpu.VMEM((mixed_blocks, HD), bf16),
-            pltpu.VMEM((wide, mixed_blocks, HD), bf16),
-            pltpu.VMEM((wide * mixed_blocks, HD), f32),
-            pltpu.VMEM((wide, out_depth), bf16),
-            pltpu.VMEM((wide, out_blocks, HD), f32),
-            pltpu.VMEM((wide, out_blocks, HD), f32),
+            pltpu.VMEM((groups, wide, mixed_blocks // groups, HD), bf16),
+            pltpu.VMEM((wide * mixed_blocks // groups, HD), f32),
+            pltpu.VMEM((wide, out_depth // groups), bf16),
+            pltpu.VMEM((PARTS, wide, out_blocks // PARTS, HD), f32),
+            pltpu.VMEM((PARTS, wide, out_blocks // PARTS, HD), f32),
             dma((4,)), dma((depth // STEP,)), dma((out_depth // STEP,)),
-            dma((narrow,)), dma((narrow,)),
             dma((1,)), dma((1,)),
+            dma((PARTS,)), dma((PARTS,)),
             dma((1,)), dma((1,)),
-            dma((1,)), dma((1,)),
-            dma((1,)), dma((1,)),
+            dma((groups,)), dma((groups,)),
+            dma((PARTS,)), dma((PARTS,)),
         ],
         compiler_params=pltpu.CompilerParams(
             collective_id=0, has_side_effects=True,
@@ -294,18 +325,18 @@
         hidden_in, norm_gain.reshape(blocks, HD), cache_lengths,
         cache_keys, cache_values, qkv_weight, out_weight,
     )
-    return hidden_in.astype(f32) + out.reshape(1, blocks * HD)
+    return out.reshape(1, blocks * HD)
 
 
 def fits(sizes, hidden_in, qkv_weight, out_weight, cache_keys):
     wide, narrow = sizes
     columns = qkv_weight.shape[1]
     groups = cache_keys.shape[2] // HD
-    if hidden_in.shape[0] != 1 or columns % HD or out_weight.shape[1] % (8 * HD):
+    if hidden_in.shape[0] != 1 or columns % HD or out_weight.shape[1] % (PARTS * 8 * HD):
         return False
     if wide % narrow or (wide // narrow) % groups or wide % 8:
         return False
-    if qkv_weight.shape[0] % STEP or out_weight.shape[0] % STEP:
+    if qkv_weight.shape[0] % (PARTS * STEP) or out_weight.shape[0] % (groups * STEP):
         return False
     queries = (wide // narrow) // groups * (columns // HD) - 2
     return queries % 16 == 0 and queries * groups * HD == out_weight.shape[0]

time: 32.9 us -> 30.2 us (0.918)
  Pallas kernels: 30.4 us -> 27.9 us
  other arithmetic: 1.42 us -> 0 us
  local copies, waits for them, and re-layouts: 0.01 us -> 1.38 us
    pallas_call x1, Pallas kernels: 30.4 us -> 27.9 us  [fused(): pl.pallas_call(functools.partial(decode_kernel, wide, narrow, heads, grou...]
    add x1 -> x0, other arithmetic: 1.42 us -> none  [fused(): return hidden_in.astype(f32) + out.reshape(1, blocks * HD)]
    unnamed x2 -> x1, local copies, waits for them, and re-layouts: 0.01 us -> 1.38 us
where the time goes in v2:
time: 30.2 us; the launch traced here: 30 us
  Pallas kernels  27.9 us (92%)
  local copies, waits for them, and re-layouts  1.38 us (5%)
  between operations  0.66 us (2%)
    pallas_call x1, Pallas kernels, fused(): pl.pallas_call(functools.partial(decode_kernel, wide, narrow, heads, grou...  27.9 us
    unnamed x1, local copies, waits for them, and re-layouts  1.38 us

profile of v2, /device:TPU:0, one launch (start us, length us, event | category | flops | bytes accessed | tf_op | source)
XLA Modules:
  0.0 30.0 jit_solution(14447653938301829186)
XLA Ops:
  0.7 27.9 %decode.1 = f32[64,128]{1,0:T(8,128)} custom-call(bf16[1,8192]{1,0:T(2,128)(2,1)} %h_hbm.1, f32[64,128]{1,0:T(8,128)} %bitcast.3, s32[1]{0:T(128)S(6)} %copy.9.len_ref, bf16[1,256,256]{2,1,0:T(8,128)(2,1)} %k_hbm.1, bf16[1,256,256]{2,1,0:T(8,128)(2,1)} %v_hbm.1, bf16[8192,1152]{1,0:T(8,128)(2,1)} %wq_hbm.1, bf16[4096,2048]{1,0:T(8,128)(2,1)} %wo_hbm.1), custom_call_target="tpu_custom_call" | custom-call | flops 285212672 | bytes 35651584 | tf_op jit(solution)/shard_map/decode/pallas_call | solution.py:277
  28.6 1.4 %copy.10 = f32[1,8192]{1,0:T(1,128)} copy(f32[1,8192]{1,0:T(1,128)} %bitcast.2) | data formatting | bytes 65536
